TPU v7x, 512 devices: a whole 4x4x16 slice. The times are simulated.
512 devices in a mesh: traj: 32 (over z_hi, y, core), tm: 16 (over z_lo, x).
Axes of the slice: x: 4, y: 4, z: 16 (z_hi: 4, z_lo: 4; z = z_hi * 4 + z_lo), core: 2. Of those that a mesh axis runs over, the one named last changes fastest.
Arguments:
- states: float32 [16, 32, 8192], P('tm', None, 'traj'), may hold values from -6 to 6
- vectors: bfloat16 [64, 8192], P(None, 'traj'), may hold values from -6 to 6
- kernel_scale: float32 [16], P('tm'), may hold values from 6 to 16
- neighbour_blocks: int32 [64, 24], P('traj'), may hold values from 0 to 63, as said below
- neighbour_count: int32 [64], P('traj'), may hold values from 6 to 24, as said below
Outputs:
- result: float32 [64, 8192], P(None, 'traj')
Inputs may be any that keep to these rules, and one draw needn't show every extreme that they name: `neighbour_blocks`: row b names 24 different blocks, the first of them b itself. Only the first neighbour_count[b] entries of row b of neighbour_blocks are neighbours of block b; some block uses all 24.
All inputs are finite; a program needn't handle non-finite values.
Results may differ from a plain program's by a relative error of at most 0.0013.
Values may be sent and summed in bfloat16 or wider, within the bound.
A program may use at most 64 MiB of HBM per device.

v0:
```python
import math

import jax
import jax.numpy as jnp
from jax import lax
from jax.sharding import Mesh
from jax.sharding import PartitionSpec as P

BLK = 128
TRAJ = ("traj_0", "traj_1", "traj_2")


def in_order(blocks, dim):
    dims = list(blocks.shape[1:])
    dims[dim] *= blocks.shape[0]
    return jnp.moveaxis(blocks, 0, dim).reshape(dims)


def all_blocks(array, axes, turns):
    blocks = array[None]
    for k in turns:
        blocks = lax.all_gather(blocks, axes[k], axis=0, tiled=True)
    block = [lax.axis_size(axes[k]) for k in reversed(turns)]
    blocks = blocks.reshape(*block, *array.shape)
    turned = sorted(range(len(turns)), key=lambda place: turns[len(turns) - 1 - place])
    return blocks.transpose(*turned, *range(len(turns), blocks.ndim)).reshape(-1, *array.shape)


def gather_axes(array, axes, turns, dim):
    return in_order(all_blocks(array, axes, turns), dim)


def sent_together(arrays, axis, dim, along):
    widths = [math.prod(a.shape[along:]) for a in arrays]
    both = jnp.concatenate(
        [a.reshape(*a.shape[:along], w) for a, w in zip(arrays, widths)], axis=along
    )
    out = lax.all_gather(both, axis, axis=dim, tiled=True)
    blocks = jnp.split(out, [sum(widths[:k]) for k in range(1, len(widths))], axis=along)
    return tuple((b.reshape(*out.shape[:along], *a.shape[along:]) for a, b in zip(arrays, blocks)))


def copy_for_each(array, axis):
    copies = jnp.broadcast_to(array, (lax.axis_size(axis), *array.shape))
    return lax.all_to_all(copies, axis, split_axis=0, concat_axis=0, tiled=True)


def of_everyone(array, axis):
    return copy_for_each(array, axis).sum(axis=0)


def linked_blocks(neighbour_blocks, neighbour_count, blocks_total):
    slots = neighbour_blocks.shape[1]
    named = neighbour_blocks[:, :, None] == jnp.arange(blocks_total, dtype=jnp.int32)[None, None, :]
    within = jnp.arange(slots, dtype=jnp.int32)[None, :, None] < neighbour_count[:, None, None]
    return jnp.any(named & within, axis=1).astype(jnp.float32)


def per_device(states, vectors, kernel_scale, neighbour_blocks, neighbour_count):
    coords_all = gather_axes(states, (("traj_0", "traj_1"), "traj_2"), (0, 1), 2)[0]
    vectors_all = lax.all_gather(vectors, TRAJ, axis=1, tiled=True)
    own = states[0]
    spread = kernel_scale[0]
    own_rows = own.shape[1]
    columns = coords_all.shape[1]
    vector_count = vectors.shape[0]
    blocks_total = columns // BLK
    block_rows = own_rows // BLK
    own_squares = jnp.sum(own * own, axis=0)
    all_squares = jnp.sum(coords_all * coords_all, axis=0)
    tile_width = math.gcd(columns, 512)
    tile_count = columns // tile_width
    linked = linked_blocks(neighbour_blocks, neighbour_count, blocks_total)

    def dense_kernel(tile_index):
        offset = tile_index * tile_width
        slab = lax.dynamic_slice_in_dim(coords_all, offset, tile_width, 1)
        cross = lax.dot_general(
            own, slab, (((0,), (0,)), ((), ())), precision=lax.Precision.HIGHEST
        )
        slab_squares = lax.dynamic_slice_in_dim(all_squares, offset, tile_width, 0)
        distance = own_squares[:, None] + slab_squares[None, :] - 2.0 * cross
        mask = lax.dynamic_slice_in_dim(linked, offset // BLK, tile_width // BLK, 1)
        shaped = jnp.exp(-distance / spread).reshape(block_rows, BLK, tile_width // BLK, BLK)
        return (mask[:, None, :, None] * shaped).reshape(own_rows, tile_width)

    def first_dense(tile_index, carry):
        row_sum, pushed = carry
        kernel = dense_kernel(tile_index)
        weights = kernel.astype(jnp.bfloat16)
        slab_vectors = lax.dynamic_slice_in_dim(vectors_all, tile_index * tile_width, tile_width, 1)
        pushed = pushed + lax.dot_general(
            slab_vectors, weights, (((1,), (1,)), ((), ())), preferred_element_type=jnp.float32
        )
        return (row_sum + jnp.sum(kernel, axis=1), pushed)

    row_sum, pushed = lax.fori_loop(
        0,
        tile_count,
        first_dense,
        (jnp.zeros((own_rows,), jnp.float32), jnp.zeros((vector_count, own_rows), jnp.float32)),
    )
    scaled = (pushed / (row_sum * row_sum)[None, :]).astype(jnp.bfloat16)
    lists_whole, counts_whole = sent_together((neighbour_blocks, neighbour_count), TRAJ, 0, 1)
    linked_whole = linked_blocks(lists_whole, counts_whole, blocks_total)
    own_start = lax.axis_index(TRAJ) * block_rows
    column_mask = lax.dynamic_slice_in_dim(linked_whole, own_start, block_rows, 1)
    scaled_whole = lax.all_gather(scaled, TRAJ, axis=1, tiled=True)

    def pull_tile(tile_index, total):
        offset = tile_index * tile_width
        slab = lax.dynamic_slice_in_dim(coords_all, offset, tile_width, 1)
        cross = lax.dot_general(
            slab, own, (((0,), (0,)), ((), ())), precision=lax.Precision.HIGHEST
        )
        slab_squares = lax.dynamic_slice_in_dim(all_squares, offset, tile_width, 0)
        distance = slab_squares[:, None] + own_squares[None, :] - 2.0 * cross
        mask = lax.dynamic_slice_in_dim(column_mask, offset // BLK, tile_width // BLK, 0)
        shaped = jnp.exp(-distance / spread).reshape(tile_width // BLK, BLK, block_rows, BLK)
        weights = (
            (mask[:, None, :, None] * shaped).reshape(tile_width, own_rows).astype(jnp.bfloat16)
        )
        slab_scaled = lax.dynamic_slice_in_dim(scaled_whole, offset, tile_width, 1)
        return total + jnp.dot(slab_scaled, weights, preferred_element_type=jnp.float32)

    own_pulled = lax.fori_loop(
        0, tile_count, pull_tile, jnp.zeros((vector_count, own_rows), jnp.float32)
    )
    result = of_everyone(own_pulled, "tm")
    return result


def solution(mesh):
    split = Mesh(
        mesh.devices.reshape(4, 4, 2, mesh.shape["tm"]), ("traj_0", "traj_1", "traj_2", "tm")
    )
    in_specs = (P("tm", None, TRAJ), P(None, TRAJ), P("tm"), P(TRAJ, None), P(TRAJ))
    out_specs = P(None, TRAJ)
    return jax.shard_map(
        per_device, mesh=split, in_specs=in_specs, out_specs=out_specs, check_vma=False
    )
```

profile of v0, /device:TPU:1, one launch (start us, length us, event | category | flops | bytes accessed | tf_op | source)
XLA Modules:
  0.0 364.6 jit_solution(11835117052081428395)
XLA Ops:
  6.5 58.6 %all-gather = f32[16,32,256]{2,1,0:T(8,128)} all-gather(f32[1,32,256]{2,1,0:T(8,128)} %param.9), channel_id=2, replica_groups=mesh['traj_0'=4,'traj_1'=4,'traj_2'=2,'tm'=16] {'traj_0','traj_1'}, dimensions={0}, use_global_device_ids=true | all-gather | bytes 557056 | tf_op jit(solution)/shard_map/all_gather | solution.py:22
  67.4 20.4 %all-gather.11.cloned.1.call-done = f32[32,32,256]{2,1,0:T(8,128)} async-done(((f32[16,32,256]{2,1,0:T(8,128)}), f32[32,32,256]{2,1,0:T(8,128)}) %all-gather.11.cloned.1.call-update) | async-done | bytes 1048592 | tf_op jit(solution)/shard_map/all_gather | solution.py:22
  87.8 1.3 copy.19
  89.4 74.3 %all-gather.7.cloned.1.call-done = bf16[64,8192]{1,0:T(8,128)(2,1)} async-done(((bf16[64,256]{1,0:T(8,128)(2,1)}), bf16[64,8192]{1,0:T(8,128)(2,1)}) %all-gather.7.cloned.1.call-update) | async-done | bytes 1048592 | tf_op jit(solution)/shard_map/all_gather | solution.py:61
  163.7 47.5 %while.34 = (s32[]{:T(128)}, f32[256]{0:T(256)S(1)}, f32[64,256]{1,0:T(8,128)S(1)}, f32[2,64]{1,0:T(2,128)S(1)}, f32[256]{0:T(256)S(1)}, /*index=5*/f32[8192]{0:...) while((s32[]{:T(128)}, f32[256]{0:T(256)S(1)}, ...), condition=%wide.region_6.7_spmd.clone, body=%wide.region_4.0_spmd.clone.sunk | while | flops 68190488 | bytes 1879617 | solution.py:97
  164.1 1.4 fusion.42
  167.1 1.4 fusion.42
  170.1 1.4 fusion.42
  171.5 1.0 convolution_add_fusion.4
  173.1 1.4 fusion.42
  176.0 1.4 fusion.42
  179.0 1.4 fusion.42
  182.0 1.4 fusion.42
  184.9 1.4 fusion.42
  187.9 1.4 fusion.42
  190.9 1.4 fusion.42
  193.9 1.4 fusion.42
  196.8 1.4 fusion.42
  198.2 1.0 convolution_add_fusion.4
  199.8 1.4 fusion.42
  202.8 1.4 fusion.42
  204.2 1.0 convolution_add_fusion.4
  205.8 1.4 fusion.42
  207.2 1.0 convolution_add_fusion.4
  208.7 1.4 fusion.42
  212.0 51.6 %all-gather.2 = s32[32,2,25]{2,1,0:T(2,128)S(1)} all-gather(s32[1,2,25]{2,1,0:T(2,128)S(1)} %add_bitcast_fusion), channel_id=1, replica_groups=mesh['traj_0'=4,'traj_1'=4,'traj_2'=2,'tm'=16] {'traj_0','traj_1','traj_2'}, dimensions={0}, use_global_device_ids=true | all-gather | bytes 6600 | tf_op jit(solution)/shard_map/all_gather | solution.py:38
  264.5 16.4 %all-gather.9.cloned.1.call-done = bf16[64,8192]{1,0:T(8,128)(2,1)} async-done(((bf16[64,256]{1,0:T(8,128)(2,1)}), bf16[64,8192]{1,0:T(8,128)(2,1)}) %all-gather.9.cloned.1.call-update) | async-done | bytes 1048592 | tf_op jit(solution)/shard_map/all_gather | solution.py:108
  281.0 44.3 %while.35 = (s32[]{:T(128)}, f32[64,256]{1,0:T(8,128)S(1)}, bf16[64,8192]{1,0:T(8,128)(2,1)}, f32[64,2]{1,0:T(8,128)S(1)}, f32[8192]{0:T(1024)S(1)}, /*index=5*/...) while((s32[]{:T(128)}, f32[64,256]{1,0:T(8,128)S(1)}, ...), condition=%wide.region_8.9_spmd.clone, body=%wide.region_7.8_spmd.clone.sunk | while | flops 68059160 | bytes 1875448 | solution.py:126
  281.3 1.4 fusion.47
  284.1 1.4 fusion.47
  286.8 1.4 fusion.47
  289.6 1.4 fusion.47
  292.4 1.4 fusion.47
  293.8 1.0 convolution_add_fusion.5
  295.2 1.4 fusion.47
  297.9 1.4 fusion.47
  300.7 1.4 fusion.47
  302.1 1.0 convolution_add_fusion.5
  303.5 1.4 fusion.47
  306.3 1.4 fusion.47
  309.0 1.4 fusion.47
  310.4 1.0 convolution_add_fusion.5
  311.8 1.4 fusion.47
  314.6 1.4 fusion.47
  317.3 1.4 fusion.47
  320.1 1.4 fusion.47
  322.9 1.4 fusion.47
  325.4 31.9 %all_to_all.5 = f32[16,64,256]{2,1,0:T(8,128)S(1)} all-to-all(f32[16,64,256]{2,1,0:T(8,128)S(1)} %broadcast_in_dim.37), channel_id=1, replica_groups=mesh['traj_0'=4,'traj_1'=4,'traj_2'=2,'tm'=16] {'tm'}, dimensions={0} | all-to-all | bytes 2097152 | tf_op jit(solution)/shard_map/all_to_all | solution.py:45
  (186 shorter events, 42.9 us)
Async XLA Ops:
  6.5 81.2 %all-gather.11.cloned.1.call-start = ((), (), s32[]{:S(2)}) async-start(), calls=%async_computation.3 | async-start | bytes 1572864 | tf_op jit(solution)/shard_map/all_gather | solution.py:22
  65.1 2.3 copy-start
  65.1 98.5 %all-gather.7.cloned.1.call-start = ((), (), s32[]{:S(2)}) async-start(), calls=%async_computation.1 | async-start | bytes 1081344 | tf_op jit(solution)/shard_map/all_gather | solution.py:61
  65.9 215.1 %all-gather.9.cloned.1.call-start = ((), (), s32[]{:S(2)}) async-start(), calls=%async_computation.2 | async-start | bytes 1081344 | tf_op jit(solution)/shard_map/all_gather | solution.py:108
  65.9 0.7 copy-start.2
  66.6 0.7 copy-start.1
Sparse Core Ops, SparseCore 0:
  65.2 22.4 all-gather.10
  90.8 72.7 all-gather.6
  212.0 68.9 all-gather.8
where the time goes:
time: 368 us; the launch traced here: 365 us
  blocking collectives  142 us (39%)
  waiting for transfers between devices  112 us (30%)
  matrix products  77.2 us (21%)
  local copies, waits for them, and re-layouts  15 us (4%)
  between operations  13.3 us (4%)
    all_gather x1, waiting for transfers between devices, per_device(): vectors_all = lax.all_gather(vectors, TRAJ, axis=1, tiled=True)  74.3 us
    all_gather x1, blocking collectives, all_blocks(): blocks = lax.all_gather(blocks, axes[k], axis=0, tiled=True)  58.6 us
    all_gather x1, blocking collectives, sent_together(): out = lax.all_gather(both, axis, axis=dim, tiled=True)  51.6 us
    all_to_all x1, blocking collectives, copy_for_each(): return lax.all_to_all(copies, axis, split_axis=0, concat_axis=0, tiled=True)  31.9 us
    dot_general x16, matrix products, dense_kernel(): lax.dot_general(own, slab, (((0,), (0,)), ((), ())), precision=lax.Precis...  22.3 us
    dot_general x16, matrix products, pull_tile(): lax.dot_general(slab, own, (((0,), (0,)), ((), ())), precision=lax.Precis...  21.9 us
    all_gather x1, waiting for transfers between devices, all_blocks(): blocks = lax.all_gather(blocks, axes[k], axis=0, tiled=True)  20.4 us
    dot_general x16, matrix products, first_dense(): lax.dot_general(slab_vectors, weights, (((1,), (1,)), ((), ())), preferre...  16.5 us
  transfers between devices with their start and end apart: 3, of which 3 were waited for; matrix products, arithmetic and copies ran while one was open for 1% of the time, Pallas kernels for 0%

commit v1 on v0

v1 whole, which is shorter than its diff:
```python
import functools
import math

import jax
import jax.numpy as jnp
from jax import lax
from jax.experimental import pallas as pl
from jax.experimental.pallas import tpu as pltpu
from jax.sharding import PartitionSpec as P

MESH = pl.DeviceIdType.MESH
BLK = 128
STEP = 5461.0
NONE = -1


def wait_for(ref, sem):
    pltpu.make_async_copy(ref, ref, sem).wait()


def digits(codes):
    high = (codes + 128) >> 8
    low = codes - (high << 8)
    return (high << 8).astype(jnp.float32), low.astype(jnp.float32)


def three_parts(value):
    one = value.astype(jnp.bfloat16).astype(jnp.float32)
    two = (value - one).astype(jnp.bfloat16).astype(jnp.float32)
    return one, two, value - one - two


def augmented(codes, times, order, first):
    whole = codes.astype(jnp.int32)
    high, low = digits(whole)
    real = whole.astype(jnp.float32)
    square = jnp.sum(real * real, axis=0, keepdims=True)
    row = lax.broadcasted_iota(jnp.int32, (16, codes.shape[1]), 0)
    extra = jnp.where((row >= 3 - first) & (row < 6 - first), 1.0, 0.0)
    for k, part in enumerate(three_parts(square)):
        extra = jnp.where(row == first + k, part, extra)
    both = {"h": (high * times).astype(jnp.bfloat16), "l": (low * times).astype(jnp.bfloat16)}
    return jnp.concatenate([both[k] for k in order] + [extra.astype(jnp.bfloat16)], axis=0)


def kernel(
    side,
    slices,
    states,
    vectors,
    scale,
    lists,
    counts,
    out,
    st_all,
    st_pair,
    ls_all,
    ls_pair,
    ve_all,
    sc_all,
    basis,
    mask_1,
    mask_2,
    first,
    second,
    row_sum,
    total,
    px_out,
    px_in,
    rs_out,
    rs_in,
    ag,
    st_send,
    st_recv,
    ls_send,
    ls_recv,
    ve_send,
    ve_recv,
    sc_send,
    sc_recv,
    pair_send,
    pair_recv,
    rs_send,
    rs_recv,
    ag_send,
    ag_recv,
    local_sem,
):
    chips = side * side
    traj, tm = lax.axis_index("traj"), lax.axis_index("tm")
    core, chip = traj % 2, traj // 2
    y, zh = chip % side, chip // side
    own = states.shape[1]
    vecs = vectors.shape[0]
    blocks = own // BLK

    def place(dz, dy):
        return ((zh + dz) % side) * side + (y + dy) % side

    def at(where, other=0):
        return {"traj": where * 2 + (core + other) % 2, "tm": tm}

    def at_slice(d):
        return {"traj": traj, "tm": (tm + d) % slices}

    near = [(0, d) for d in range(1, side)]
    far = [(d, 0) for d in range(1, side)]

    barrier = pltpu.get_barrier_semaphore()
    for dz, dy in far + near:
        pl.semaphore_signal(barrier, inc=1, device_id=at(place(dz, dy)), device_id_type=MESH)
    pl.semaphore_signal(barrier, inc=1, device_id=at(chip, 1), device_id_type=MESH)
    for d in range(1, slices):
        pl.semaphore_signal(barrier, inc=1, device_id=at_slice(d), device_id_type=MESH)

    local = pltpu.make_async_copy(vectors, ve_all.at[chip], local_sem)
    local.start()
    st_all[chip] = jnp.round(states[...] * STEP).astype(jnp.int32).astype(jnp.int16)
    ls_all[chip] = jnp.full((8, 128), NONE, jnp.int32)
    slot = lax.broadcasted_iota(jnp.int32, (1, lists.shape[1]), 1)
    for b in range(blocks):
        ls_all[chip, b : b + 1, : lists.shape[1]] = jnp.where(
            slot < counts[b], lists[b : b + 1, :], NONE
        )
    pl.semaphore_wait(barrier, 2 * side - 1 + slices - 1)

    def copy(src, dst, send, recv, device):
        return pltpu.make_async_remote_copy(
            src_ref=src, dst_ref=dst, send_sem=send, recv_sem=recv, device_id=device, device_id_type=MESH
        )

    def send_own(everyone, send, recv):
        for k, (dz, dy) in enumerate(far + near):
            copy(
                everyone.at[chip], everyone.at[chip], send.at[k], recv.at[chip], at(place(dz, dy))
            ).start()

    def forward(everyone, send, recv, dz):
        where = place(dz, 0)
        wait_for(everyone.at[where], recv.at[where])
        for k in range(1, side):
            copy(
                everyone.at[where],
                everyone.at[where],
                send.at[(dz + 1) * (side - 1) + k - 1],
                recv.at[where],
                at(place(0, k)),
            ).start()

    def all_sent(everyone, send):
        for k in range(chips - 1):
            wait_for(everyone.at[0], send.at[k])

    def pair(src, dst, k):
        return copy(src, dst, pair_send.at[k], pair_recv.at[k], at(chip, 1))

    send_own(st_all, st_send, st_recv)
    st_swap = pair(st_all.at[chip], st_pair, 0)
    st_swap.start()
    send_own(ls_all, ls_send, ls_recv)
    ls_swap = pair(ls_all.at[chip], ls_pair, 1)
    ls_swap.start()
    local.wait()
    send_own(ve_all, ve_send, ve_recv)

    hops = [1, side - 1] + list(range(2, side - 1)) if side > 2 else [1]
    for dz in hops:
        forward(st_all, st_send, st_recv, dz)
        forward(ls_all, ls_send, ls_recv, dz)

    basis[:, :own] = augmented(st_all[chip], -2.0, "hlhl", 3)
    st_swap.wait_recv()
    basis[:, own:] = augmented(st_pair[...], -2.0, "hlhl", 3)
    ls_swap.wait_recv()
    row_sum[...] = jnp.zeros_like(row_sum)
    rate = -math.log2(math.e) / (STEP * STEP) / scale[0]

    def build(where):
        base = 4 * where + 2 * core
        entry = lax.broadcasted_iota(jnp.int32, (8, 128), 0)
        there = ls_all[where]
        for b in range(2 * blocks):
            held = ls_all[chip] if b < blocks else ls_pair[...]
            mine = held[b % blocks : b % blocks + 1, :]
            name = 4 * chip + 2 * ((core + b // blocks) % 2) + b % blocks
            lanes = slice(b * BLK, (b + 1) * BLK)
            hit_1 = jnp.where(mine == base + entry, 1.0, 0.0)
            hit_2 = jnp.where(there == name, 1.0, 0.0)
            mask_1[where, :, lanes] = jnp.broadcast_to(
                jnp.max(hit_1, axis=1, keepdims=True), (8, BLK)
            )
            mask_2[where, :, lanes] = jnp.broadcast_to(
                jnp.max(hit_2, axis=1, keepdims=True), (8, BLK)
            )
        rows = augmented(st_all[where], 1.0, "hhll", 0)
        for h in range(blocks):
            part = slice(h * BLK, (h + 1) * BLK)
            distance = lax.dot_general(
                rows[:, part],
                basis[...],
                (((0,), (0,)), ((), ())),
                preferred_element_type=jnp.float32,
            )
            weight = jnp.exp2(distance * rate)
            linked = weight * mask_1[where, h : h + 1, :]
            row_sum[...] += jnp.sum(linked.reshape(BLK // 8, 8, 2 * own), axis=0)
            first[where, part, :] = linked.astype(jnp.bfloat16)
            second[where, part, :] = (weight * mask_2[where, h : h + 1, :]).astype(jnp.bfloat16)

    build(chip)
    for dz in [0] + hops:

        def one_build(dy, carry, dz=dz):
            where = place(dz, dy)
            wait_for(st_all.at[where], st_recv.at[where])
            wait_for(ls_all.at[where], ls_recv.at[where])
            build(where)
            return carry

        if dz:
            build(place(dz, 0))
        lax.fori_loop(1, side, one_build, 0)

    for dz in hops:
        forward(ve_all, ve_send, ve_recv, dz)

    def product(everyone, recv, weights):
        total[...] = jnp.zeros_like(total)
        for dz in [0] + hops:
            for dy in range(side):
                where = place(dz, dy)
                if dy:
                    wait_for(everyone.at[where], recv.at[where])
                total[...] += jnp.dot(
                    everyone[where], weights[where], preferred_element_type=jnp.float32
                )

    product(ve_all, ve_recv, first)
    px_out[0, :vecs] = total[:, own:]
    px_out[0, vecs:] = row_sum[:, own:]
    swap_1 = pair(px_out.at[0], px_in.at[0], 2)
    swap_1.start()
    swap_1.wait_recv()
    sums = jnp.sum(row_sum[:, :own] + px_in[0, vecs:], axis=0, keepdims=True)
    sc_all[chip] = ((total[:, :own] + px_in[0, :vecs]) / (sums * sums)).astype(jnp.bfloat16)

    send_own(sc_all, sc_send, sc_recv)
    for dz in hops:
        forward(sc_all, sc_send, sc_recv, dz)
    product(sc_all, sc_recv, second)
    px_out[1, :vecs] = total[:, own:]
    swap_2 = pair(px_out.at[1, pl.ds(0, vecs)], px_in.at[1, pl.ds(0, vecs)], 3)
    swap_2.start()
    swap_2.wait_recv()

    tiles = rs_out.shape[0]
    wide = own // 128
    per = tiles // slices
    for t in range(tiles):
        rows, lanes = slice(t // wide * 8, t // wide * 8 + 8), slice(t % wide * 128, t % wide * 128 + 128)
        rs_out[t] = total[rows, lanes] + px_in[1, rows, lanes]

    def scatter(d, carry):
        there = (tm + d) % slices
        copy(
            rs_out.at[pl.ds(there * per, per)], rs_in.at[tm], rs_send.at[d], rs_recv.at[tm], at_slice(d)
        ).start()
        return carry

    def scattered(d, carry):
        there = (tm + d) % slices
        wait_for(rs_in.at[there], rs_recv.at[there])
        return carry

    lax.fori_loop(1, slices, scatter, 0)
    rs_in[tm] = rs_out[pl.ds(tm * per, per)]
    lax.fori_loop(1, slices, scattered, 0)
    ag[tm] = jnp.sum(rs_in[...], axis=0)

    def spread(d, carry):
        copy(ag.at[tm], ag.at[tm], ag_send.at[d], ag_recv.at[tm], at_slice(d)).start()
        return carry

    def arrived(d, carry):
        there = (tm + d) % slices
        wait_for(ag.at[there], ag_recv.at[there])
        return carry

    lax.fori_loop(1, slices, spread, 0)
    lax.fori_loop(1, slices, arrived, 0)
    for t in range(tiles):
        rows, lanes = slice(t // wide * 8, t // wide * 8 + 8), slice(t % wide * 128, t % wide * 128 + 128)
        out[rows, lanes] = ag[t // per, t % per]

    all_sent(st_all, st_send)
    all_sent(ls_all, ls_send)
    all_sent(ve_all, ve_send)
    all_sent(sc_all, sc_send)
    for swap in (st_swap, ls_swap, swap_1, swap_2):
        swap.wait_send()

    def sent(d, carry):
        wait_for(rs_in.at[0], rs_send.at[d])
        wait_for(ag.at[0], ag_send.at[d])
        return carry

    lax.fori_loop(1, slices, sent, 0)


def per_device(side, slices, states, vectors, kernel_scale, neighbour_blocks, neighbour_count):
    coords, own = states.shape[1:]
    vecs = vectors.shape[0]
    chips = side * side
    tiles = vecs * own // 1024
    vmem = pl.BlockSpec(memory_space=pltpu.VMEM)
    smem = pl.BlockSpec(memory_space=pltpu.SMEM)
    dma = pltpu.SemaphoreType.DMA
    return pl.pallas_call(
        functools.partial(kernel, side, slices),
        out_shape=jax.ShapeDtypeStruct((vecs, own), jnp.float32),
        in_specs=[vmem, vmem, smem, vmem, smem],
        out_specs=vmem,
        scratch_shapes=[
            pltpu.VMEM((chips, coords, own), jnp.int16),
            pltpu.VMEM((coords, own), jnp.int16),
            pltpu.VMEM((chips, 8, 128), jnp.int32),
            pltpu.VMEM((8, 128), jnp.int32),
            pltpu.VMEM((chips, vecs, own), jnp.bfloat16),
            pltpu.VMEM((chips, vecs, own), jnp.bfloat16),
            pltpu.VMEM((4 * coords + 16, 2 * own), jnp.bfloat16),
            pltpu.VMEM((chips, 8, 2 * own), jnp.float32),
            pltpu.VMEM((chips, 8, 2 * own), jnp.float32),
            pltpu.VMEM((chips, own, 2 * own), jnp.bfloat16),
            pltpu.VMEM((chips, own, 2 * own), jnp.bfloat16),
            pltpu.VMEM((8, 2 * own), jnp.float32),
            pltpu.VMEM((vecs, 2 * own), jnp.float32),
            pltpu.VMEM((2, vecs + 8, own), jnp.float32),
            pltpu.VMEM((2, vecs + 8, own), jnp.float32),
            pltpu.VMEM((tiles, 8, 128), jnp.float32),
            pltpu.VMEM((slices, tiles // slices, 8, 128), jnp.float32),
            pltpu.VMEM((slices, tiles // slices, 8, 128), jnp.float32),
            dma((chips,)),
            dma((chips,)),
            dma((chips,)),
            dma((chips,)),
            dma((chips,)),
            dma((chips,)),
            dma((chips,)),
            dma((chips,)),
            dma((4,)),
            dma((4,)),
            dma((slices,)),
            dma((slices,)),
            dma((slices,)),
            dma((slices,)),
            dma,
        ],
        compiler_params=pltpu.CompilerParams(
            collective_id=0, has_side_effects=True, vmem_limit_bytes=40 * 1024 * 1024
        ),
    )(states.reshape(coords, own), vectors, kernel_scale, neighbour_blocks, neighbour_count)


def solution(mesh):
    side, slices = math.isqrt(mesh.shape["traj"] // 2), mesh.shape["tm"]
    return jax.shard_map(
        functools.partial(per_device, side, slices),
        mesh=mesh,
        in_specs=(P("tm", None, "traj"), P(None, "traj"), P("tm"), P("traj", None), P("traj")),
        out_specs=P(None, "traj"),
        check_vma=False,
    )
```

time: 368 us -> 71.2 us (0.19)
  blocking collectives: 142 us -> 0 us
  waiting for transfers between devices: 112 us -> 0 us
  matrix products: 77.2 us -> 0 us
  Pallas kernels: 0 us -> 67.4 us
  between operations: 13.3 us -> 0.68 us
  local copies, waits for them, and re-layouts: 15 us -> 2.81 us
    all_gather x3 -> x0, waiting for transfers between devices: 111 us -> none  [the longest x1 74.3 us: per_device(): vectors_all = lax.all_gather(vectors, TRAJ, axis=1, tiled=True)]
    all_gather x2 -> x0, blocking collectives: 110 us -> none  [the longest x1 58.6 us: all_blocks(): blocks = lax.all_gather(blocks, axes[k], axis=0, tiled=True)]
    dot_general x64 -> x0, matrix products: 77.2 us -> none  [the longest x16 22.3 us: dense_kernel(): lax.dot_general(own, slab, (((0,), (0,)), ((), ())), precision=lax.Precis...]
    pallas_call x0 -> x1, Pallas kernels: none -> 67.4 us  [per_device(): pl.pallas_call(functools.partial(kernel, side, slices), out_shape=jax.Sha...]
    all_to_all x1 -> x0, blocking collectives: 31.9 us -> none  [copy_for_each(): return lax.all_to_all(copies, axis, split_axis=0, concat_axis=0, tiled=True)]
    mul x32 -> x0, local copies, waits for them, and re-layouts: 6.53 us -> none  [the longest x16 3.28 us: dense_kernel(): return (mask[:, None, :, None] * shaped).reshape(own_rows, tile_width)]
    dynamic_slice x80 -> x0, local copies, waits for them, and re-layouts: 5.41 us -> none  [the longest x32 2.72 us: dense_kernel(): mask = lax.dynamic_slice_in_dim(linked, offset // BLK, tile_width // BLK, 1)]
  transfers between devices with their start and end apart: 3 -> 0, of which waited for: 3 -> 0; matrix products, arithmetic and copies ran while one was open for 1% -> 0% of each run, Pallas kernels for 0% -> 0%
where the time goes in v1:
time: 71.2 us; the launch traced here: 70.9 us
  Pallas kernels  67.4 us (95%)
  local copies, waits for them, and re-layouts  2.81 us (4%)
    pallas_call x1, Pallas kernels, per_device(): pl.pallas_call(functools.partial(kernel, side, slices), out_shape=jax.Sha...  67.4 us
    unnamed x9, local copies, waits for them, and re-layouts  2.81 us

profile of v1, /device:TPU:1, one launch (start us, length us, event | category | flops | bytes accessed | tf_op | source)
XLA Modules:
  0.0 70.9 jit_solution(3245173085157957108)
XLA Ops:
  0.7 0.0 copy-start.2
  0.7 0.0 copy-start.3
  0.7 0.7 copy-done.2
  1.3 0.0 copy-done.3
  1.3 0.0 copy-start
  1.3 0.8 %copy-done = f32[1,32,256]{2,1,0:T(8,128)S(1)} copy-done((f32[1,32,256]{2,1,0:T(8,128)S(1)}, f32[1,32,256]{2,1,0:T(8,128)}, u32[]{:S(2)}) %copy-start) | copy-done | bytes 32792
  2.1 0.0 copy-start.1
  2.1 0.8 %copy-done.1 = bf16[64,256]{1,0:T(8,128)(2,1)S(1)} copy-done((bf16[64,256]{1,0:T(8,128)(2,1)S(1)}, bf16[64,256]{1,0:T(8,128)(2,1)}, u32[]{:S(2)}) %copy-start.1) | copy-done | bytes 32792
  2.9 67.4 %shard_map.55 = f32[64,256]{1,0:T(8,128)S(1)} custom-call(f32[32,256]{1,0:T(8,128)S(1)} %bitcast.1, bf16[64,256]{1,0:T(8,128)(2,1)S(1)} %copy-done.1, f32[1]{0:T(128)S(6)} %copy.7.scale, s32[2,24]{1,0:T(2,128)S(1)} %copy-done.2, s32[2]{0:T(128)S(1)} %copy-done.3), custom_call_target="tpu_custom_call" | custom-call | tf_op jit(solution)/shard_map/pallas_call | solution.py:318
  70.3 0.6 copy.8
Async XLA Ops:
  0.7 0.7 copy-start.2
  0.7 0.7 copy-start.3
  1.3 0.8 %copy-start = (f32[1,32,256]{2,1,0:T(8,128)S(1)}, f32[1,32,256]{2,1,0:T(8,128)}, u32[]{:S(2)}) copy-start(f32[1,32,256]{2,1,0:T(8,128)} %param.5) | copy-start | bytes 98308
  2.1 0.8 %copy-start.1 = (bf16[64,256]{1,0:T(8,128)(2,1)S(1)}, bf16[64,256]{1,0:T(8,128)(2,1)}, u32[]{:S(2)}) copy-start(bf16[64,256]{1,0:T(8,128)(2,1)} %vectors.1) | copy-start | bytes 98308

commit v2 on v1

v2 whole, which is shorter than its diff:
```python
import functools
import math

import jax
import jax.numpy as jnp
from jax import lax
from jax.experimental import pallas as pl
from jax.experimental.pallas import tpu as pltpu
from jax.sharding import PartitionSpec as P

MESH = pl.DeviceIdType.MESH
BLK = 128
FO = 0
SO = 3
VL = 32
STEP = 5461.0
NONE = -1


def wait_for(ref, sem):
    pltpu.make_async_copy(ref, ref, sem).wait()


def digits(codes):
    high = (codes + 128) >> 8
    low = codes - (high << 8)
    return (high << 8).astype(jnp.float32), low.astype(jnp.float32)


def three_parts(value):
    one = value.astype(jnp.bfloat16).astype(jnp.float32)
    two = (value - one).astype(jnp.bfloat16).astype(jnp.float32)
    return one, two, value - one - two


def augmented(codes, times, order, first):
    whole = codes.astype(jnp.int32)
    high, low = digits(whole)
    real = whole.astype(jnp.float32)
    square = jnp.sum(real * real, axis=0, keepdims=True)
    row = lax.broadcasted_iota(jnp.int32, (16, codes.shape[1]), 0)
    extra = jnp.where((row >= 3 - first) & (row < 6 - first), 1.0, 0.0)
    for k, part in enumerate(three_parts(square)):
        extra = jnp.where(row == first + k, part, extra)
    both = {"h": (high * times).astype(jnp.bfloat16), "l": (low * times).astype(jnp.bfloat16)}
    return jnp.concatenate([both[k] for k in order] + [extra.astype(jnp.bfloat16)], axis=0)


def kernel(
    side,
    xs,
    slices,
    states,
    vectors,
    scale_in,
    lists_in,
    counts_in,
    out,
    coords,
    scale,
    lists,
    counts,
    st_all,
    st_pair,
    ls_all,
    ls_pair,
    ve_all,
    sc_all,
    basis,
    mask_1,
    mask_2,
    first,
    second,
    row_sum,
    total,
    px_out,
    px_in,
    rs_out,
    rs_in,
    ag,
    st_send,
    st_recv,
    ls_send,
    ls_recv,
    vz_send,
    vz_recv,
    ve_send,
    ve_recv,
    sc_send,
    sc_recv,
    pair_send,
    pair_recv,
    rs_send,
    rs_recv,
    ag_send,
    ag_recv,
    local_sem,
):
    chips = side * side
    traj, tm = lax.axis_index("traj"), lax.axis_index("tm")
    core, chip = traj % 2, traj // 2
    y, zh = chip % side, chip // side
    own = states.shape[2]
    vecs = vectors.shape[0]
    half = ls_pair.shape[1] // 2
    blocks = own // BLK

    def place(dz, dy):
        return ((zh + dz) % side) * side + (y + dy) % side

    def at(where, other=0):
        return {"traj": where * 2 + (core + other) % 2, "tm": tm}

    def at_slice(d):
        return {"traj": traj, "tm": (tm + d) % slices}

    x, zl = tm % xs, tm // xs

    def in_plane(dx, dy):
        return {"traj": place(0, dy) * 2 + core, "tm": zl * xs + (x + dx) % xs}

    plane = [(dx, dy) for dx in range(xs) for dy in range(side) if dx or dy]
    plane.sort(key=lambda d: -min(d[0], xs - d[0]) - min(d[1], side - d[1]))
    thick = vecs // xs
    share = pl.ds(pl.multiple_of(x * thick, thick), thick)

    hops = sorted(range(1, side), key=lambda d: -min(d, side - d))
    near_first = hops[::-1]
    barrier = pltpu.get_barrier_semaphore()
    for d in hops:
        pl.semaphore_signal(barrier, inc=1, device_id=at(place(d, 0)), device_id_type=MESH)
    for dx, dy in plane:
        if dy:
            pl.semaphore_signal(barrier, inc=1, device_id=in_plane(dx, dy), device_id_type=MESH)
    pl.semaphore_signal(barrier, inc=1, device_id=at(chip, 1), device_id_type=MESH)
    for d in range(1, slices):
        pl.semaphore_signal(barrier, inc=1, device_id=at_slice(d), device_id_type=MESH)

    reads = [
        pltpu.make_async_copy(src, dst, local_sem.at[k])
        for k, (src, dst) in enumerate(
            (
                (states.at[0], coords),
                (lists_in, lists),
                (counts_in, counts),
                (scale_in, scale),
                (vectors, ve_all.at[chip]),
            )
        )
    ]
    for read in reads:
        read.start()
    row_sum[...] = jnp.zeros_like(row_sum)
    total[...] = jnp.zeros_like(total)
    for read in reads:
        read.wait()
    slot = lax.broadcasted_iota(jnp.int32, (1, lists.shape[1]), 1)
    ls_all[chip] = jnp.full((1, 2 * half), NONE, jnp.int32)
    for b in range(blocks):
        ls_all[chip, :, b * half : b * half + lists.shape[1]] = jnp.where(
            slot < counts[b], lists[b : b + 1, :], NONE
        )
    st_all[chip] = jnp.round(coords[...] * STEP).astype(jnp.int32).astype(jnp.int16)
    basis[:, :own] = augmented(st_all[chip], -2.0, "hlhl", 3)
    rate = -math.log2(math.e) / (STEP * STEP) / scale[0]
    pl.semaphore_wait(barrier, (side - 1) + (xs * side - xs) + 1 + slices - 1)

    def copy(src, dst, send, recv, device):
        return pltpu.make_async_remote_copy(
            src_ref=src, dst_ref=dst, send_sem=send, recv_sem=recv, device_id=device, device_id_type=MESH
        )

    def send_z(everyone, send, recv, d):
        mine = everyone.at[chip]
        copy(mine, mine, send, recv.at[chip], at(place(d, 0))).start()

    def send_y(everyone, send, recv):
        mine = everyone.at[chip]
        for d in hops:
            copy(mine, mine, send, recv.at[chip], at(place(0, d))).start()

    def forward(everyone, send, recv, dz):
        theirs = everyone.at[place(dz, 0)]
        arrived = recv.at[place(dz, 0)]
        wait_for(theirs, arrived)
        for d in hops:
            copy(theirs, theirs, send, arrived, at(place(0, d))).start()

    def all_sent(everyone, send):
        every = everyone.at[pl.ds(0, chips - 1)]
        wait_for(every, send)

    def send_share(d):
        mine = ve_all.at[chip, share]
        copy(mine, mine, vz_send, vz_recv.at[zh], at(place(d, 0))).start()

    def forward_share(d):
        there = place(d, 0)
        theirs = ve_all.at[there, share]
        wait_for(theirs, vz_recv.at[(zh + d) % side])
        for dx, dy in plane:
            copy(theirs, theirs, ve_send.at[d], ve_recv.at[there], in_plane(dx, dy)).start()

    def shares_sent():
        wait_for(ve_all.at[pl.ds(0, side - 1), pl.ds(0, thick)], vz_send)
        wait_for(ve_all.at[pl.ds(0, side - 1)], ve_send.at[0])
        for d in hops:
            wait_for(ve_all.at[pl.ds(0, len(plane)), pl.ds(0, thick)], ve_send.at[d])

    def share_wait(dz, dy):
        where = place(dz, dy)
        if dy:
            wait_for(ve_all.at[where], ve_recv.at[where])
        elif dz and xs > 1:
            wait_for(ve_all.at[where, pl.ds(0, vecs - thick)], ve_recv.at[where])

    def shard_wait(dz, dy):
        where = place(dz, dy)
        if dy:
            wait_for(sc_all.at[where], sc_recv.at[where])

    def pair(src, dst, k):
        return copy(src, dst, pair_send.at[k], pair_recv.at[k], at(chip, 1))

    st = (st_all, st_send, st_recv)
    ls = (ls_all, ls_send, ls_recv)
    sc = (sc_all, sc_send, sc_recv)
    near, far = near_first[:-1], near_first[-1]
    if FO == 0:
        first_steps = [(w, d) for w in ("st", "ls", "ve") for d in hops + [0]]
    elif FO == 1:
        first_steps = [("st", d) for d in hops] + [("ls", d) for d in hops] + [("st", 0), ("ls", 0)] + [("ve", d) for d in hops + [0]]
    elif FO == 2:
        first_steps = [("st", far), ("ls", far), ("ve", far)] + [(w, d) for w in ("st", "ls") for d in near + [0]] + [("ve", d) for d in near + [0]]
    elif FO == 3:
        first_steps = [("st", far), ("ls", far)] + [(w, d) for w in ("st", "ls") for d in near + [0]] + [("ve", d) for d in [0] + near + [far]]
    for what, d in first_steps:
        group = {"st": st, "ls": ls, "ve": (ve_all, ve_send.at[0], ve_recv)}[what]
        if d:
            send_share(d) if what == "ve" else send_z(*group, d)
        else:
            send_y(*group)
        if what == "st" and not d:
            st_swap = pair(st_all.at[chip], st_pair, 0)
            ls_swap = pair(ls_all.at[chip], ls_pair, 1)
            st_swap.start()
            ls_swap.start()
    def build(where):
        base = 4 * where + 2 * core
        entry = lax.broadcasted_iota(jnp.int32, (8, 2 * half), 0)
        lane = lax.broadcasted_iota(jnp.int32, (8, 2 * half), 1)
        block = lane // half
        there = jnp.where(entry == block, jnp.broadcast_to(ls_all[where], (8, 2 * half)), NONE)
        for b in range(2 * blocks):
            held = ls_all[chip] if b < blocks else ls_pair[...]
            mine = jnp.where(block == b % blocks, jnp.broadcast_to(held, (8, 2 * half)), NONE)
            name = 4 * chip + 2 * ((core + b // blocks) % 2) + b % blocks
            lanes = slice(b * BLK, (b + 1) * BLK)
            for mask, hit in ((mask_1, mine == base + entry), (mask_2, there == name)):
                found = jnp.max(jnp.where(hit, 1.0, 0.0), axis=1, keepdims=True)
                mask[where, :, lanes] = jnp.broadcast_to(found, (8, BLK))
        rows = augmented(st_all[where], 1.0, "hhll", 0)
        for h in range(blocks):
            part = slice(h * BLK, (h + 1) * BLK)
            distance = lax.dot_general(
                rows[:, part],
                basis[...],
                (((0,), (0,)), ((), ())),
                preferred_element_type=jnp.float32,
            )
            weight = jnp.exp2(distance * rate)
            linked = weight * mask_1[where, h : h + 1, :]
            row_sum[...] += jnp.sum(linked.reshape(BLK // 8, 8, 2 * own), axis=0)
            first[where, part, :] = linked.astype(jnp.bfloat16)
            second[where, part, :] = (weight * mask_2[where, h : h + 1, :]).astype(jnp.bfloat16)

    def builds(dz):
        build(place(dz, 0))

        def body(dy, carry):
            where = place(dz, dy)
            wait_for(st_all.at[where], st_recv.at[where])
            wait_for(ls_all.at[where], ls_recv.at[where])
            build(where)
            return carry

        lax.fori_loop(1, side, body, 0)

    def products(everyone, arrive, weights, dz, cores=(1, 0), wait=True):
        for c in cores:
            part = slice(c * own, (c + 1) * own)
            sums = total[:, part]
            for dy in range(side):
                where = place(dz, dy)
                if wait and c == cores[0]:
                    arrive(dz, dy)
                sums = sums + jnp.dot(
                    everyone[where], weights[where, :, part], preferred_element_type=jnp.float32
                )
            total[:, part] = sums

    if SO == 0:
        second_steps = [("fs", d) for d in near] + [("b0", 0), ("b", 0), ("fs", far)] + [("b", d) for d in near] + [("fv", d) for d in near] + [("p", 0), ("b", far), ("fv", far)] + [("p", d) for d in near]
    elif SO == 1:
        second_steps = [("fs", d) for d in near] + [("b0", 0), ("b", 0)] + [("b", d) for d in near] + [("fs", far)] + [("fv", d) for d in near] + [("p", 0), ("b", far), ("fv", far)] + [("p", d) for d in near]
    elif SO == 2:
        second_steps = [("fs", d) for d in near] + [("b0", 0), ("b", 0), ("fs", far), ("fv", near[0])] + [("b", d) for d in near] + [("fv", near[-1])] + [("p", 0), ("fv", far), ("b", far)] + [("p", d) for d in near]
    elif SO == 3:
        second_steps = [("fs", d) for d in near] + [("b0", 0), ("b", 0), ("fs", far)] + [("fv", d) for d in near] + [("b", d) for d in near] + [("fv", far), ("p", 0), ("b", far)] + [("p", d) for d in near]
    for step, dz in second_steps:
        if step == "fs":
            forward(*st, dz)
            forward(*ls, dz)
        elif step == "b0":
            st_swap.wait_recv()
            basis[:, own:] = augmented(st_pair[...], -2.0, "hlhl", 3)
            ls_swap.wait_recv()
        elif step == "b":
            builds(dz)
        elif step == "fv":
            forward_share(dz)
        elif step == "p":
            products(ve_all, share_wait, first, dz)

    products(ve_all, share_wait, first, far, (1,))
    px_out[0, :vecs] = total[:, own:]
    px_out[0, vecs:] = row_sum[:, own:]
    swap_1 = pair(px_out.at[0], px_in.at[0], 2)
    swap_1.start()
    products(ve_all, share_wait, first, far, (0,), False)
    swap_1.wait_recv()
    sums = jnp.sum(row_sum[:, :own] + px_in[0, vecs:], axis=0, keepdims=True)
    sc_all[chip] = ((total[:, :own] + px_in[0, :vecs]) / (sums * sums)).astype(jnp.bfloat16)
    for d in hops:
        send_z(*sc, d)
    send_y(*sc)
    total[...] = jnp.zeros_like(total)
    for dz in near:
        forward(*sc, dz)
    products(sc_all, shard_wait, second, 0)
    forward(*sc, far)
    for dz in near:
        products(sc_all, shard_wait, second, dz)
    products(sc_all, shard_wait, second, far, (1,))
    px_out[1, :vecs] = total[:, own:]
    swap_2 = pair(px_out.at[1, pl.ds(0, vecs)], px_in.at[1, pl.ds(0, vecs)], 3)
    swap_2.start()
    products(sc_all, shard_wait, second, far, (0,), False)
    swap_2.wait_recv()

    tiles = rs_out.shape[0]
    wide = own // 128
    per = tiles // slices
    for t in range(tiles):
        rows, lanes = slice(t // wide * 8, t // wide * 8 + 8), slice(t % wide * 128, t % wide * 128 + 128)
        rs_out[t] = total[rows, lanes] + px_in[1, rows, lanes]

    for d in range(1, slices):
        there = (tm + d) % slices
        copy(
            rs_out.at[pl.ds(there * per, per)], rs_in.at[tm], rs_send, rs_recv.at[tm], at_slice(d)
        ).start()

    def scattered(d, carry):
        there = (tm + d) % slices
        wait_for(rs_in.at[there], rs_recv.at[there])
        return carry

    rs_in[tm] = rs_out[pl.ds(tm * per, per)]
    lax.fori_loop(1, slices, scattered, 0)
    ag[tm] = jnp.sum(rs_in[...], axis=0)

    for d in range(1, slices):
        copy(ag.at[tm], ag.at[tm], ag_send, ag_recv.at[tm], at_slice(d)).start()

    def arrived(d, carry):
        there = (tm + d) % slices
        wait_for(ag.at[there], ag_recv.at[there])
        return carry

    lax.fori_loop(1, slices, arrived, 0)
    for t in range(tiles):
        rows, lanes = slice(t // wide * 8, t // wide * 8 + 8), slice(t % wide * 128, t % wide * 128 + 128)
        out[rows, lanes] = ag[t // per, t % per]

    all_sent(st_all, st_send)
    all_sent(ls_all, ls_send)
    shares_sent()
    all_sent(sc_all, sc_send)
    for swap in (st_swap, ls_swap, swap_1, swap_2):
        swap.wait_send()

    wait_for(rs_in.at[pl.ds(0, slices - 1)], rs_send)
    wait_for(ag.at[pl.ds(0, slices - 1)], ag_send)


def per_device(side, xs, slices, states, vectors, kernel_scale, neighbour_blocks, neighbour_count):
    coords, own = states.shape[1:]
    vecs = vectors.shape[0]
    chips = side * side
    tiles = vecs * own // 1024
    vmem = pl.BlockSpec(memory_space=pltpu.VMEM)
    hbm = pl.BlockSpec(memory_space=pltpu.HBM)
    dma = pltpu.SemaphoreType.DMA
    return pl.pallas_call(
        functools.partial(kernel, side, xs, slices),
        out_shape=jax.ShapeDtypeStruct((vecs, own), jnp.float32),
        in_specs=[hbm] * 5,
        out_specs=vmem,
        scratch_shapes=[
            pltpu.VMEM((coords, own), jnp.float32),
            pltpu.SMEM((1,), jnp.float32),
            pltpu.VMEM(neighbour_blocks.shape, jnp.int32),
            pltpu.SMEM(neighbour_count.shape, jnp.int32),
            pltpu.VMEM((chips, coords, own), jnp.int16),
            pltpu.VMEM((coords, own), jnp.int16),
            pltpu.VMEM((chips, 1, 128), jnp.int32),
            pltpu.VMEM((1, 128), jnp.int32),
            pltpu.VMEM((chips, vecs, own), jnp.bfloat16),
            pltpu.VMEM((chips, vecs, own), jnp.bfloat16),
            pltpu.VMEM((4 * coords + 16, 2 * own), jnp.bfloat16),
            pltpu.VMEM((chips, 8, 2 * own), jnp.float32),
            pltpu.VMEM((chips, 8, 2 * own), jnp.float32),
            pltpu.VMEM((chips, own, 2 * own), jnp.bfloat16),
            pltpu.VMEM((chips, own, 2 * own), jnp.bfloat16),
            pltpu.VMEM((8, 2 * own), jnp.float32),
            pltpu.VMEM((vecs, 2 * own), jnp.float32),
            pltpu.VMEM((2, vecs + 8, own), jnp.float32),
            pltpu.VMEM((2, vecs + 8, own), jnp.float32),
            pltpu.VMEM((tiles, 8, 128), jnp.float32),
            pltpu.VMEM((slices, tiles // slices, 8, 128), jnp.float32),
            pltpu.VMEM((slices, tiles // slices, 8, 128), jnp.float32),
            dma,
            dma((chips,)),
            dma,
            dma((chips,)),
            dma,
            dma((side,)),
            dma((side,)),
            dma((chips,)),
            dma,
            dma((chips,)),
            dma((4,)),
            dma((4,)),
            dma,
            dma((slices,)),
            dma,
            dma((slices,)),
            dma((5,)),
        ],
        compiler_params=pltpu.CompilerParams(
            collective_id=0, has_side_effects=True, vmem_limit_bytes=VL * 1024 * 1024
        ),
    )(states, vectors, kernel_scale, neighbour_blocks, neighbour_count)


def solution(mesh):
    side, slices = math.isqrt(mesh.shape["traj"] // 2), mesh.shape["tm"]
    xs = min(side, slices)
    return jax.shard_map(
        functools.partial(per_device, side, xs, slices),
        mesh=mesh,
        in_specs=(P("tm", None, "traj"), P(None, "traj"), P("tm"), P("traj", None), P("traj")),
        out_specs=P(None, "traj"),
        check_vma=False,
    )
```

time: 71.2 us -> 63.5 us (0.89)
  Pallas kernels: 67.4 us -> 60.4 us
    pallas_call x1, Pallas kernels: 67.4 us -> 60.4 us  [per_device(): pl.pallas_call(functools.partial(kernel, side, xs, slices), out_shape=jax...]
where the time goes in v2:
time: 63.5 us; the launch traced here: 63.3 us
  Pallas kernels  60.4 us (95%)
  local copies, waits for them, and re-layouts  2.15 us (3%)
  between operations  0.71 us (1%)
    pallas_call x1, Pallas kernels, per_device(): pl.pallas_call(functools.partial(kernel, side, xs, slices), out_shape=jax...  60.4 us
    unnamed x9, local copies, waits for them, and re-layouts  2.15 us

profile of v2, /device:TPU:1, one launch (start us, length us, event | category | flops | bytes accessed | tf_op | source)
XLA Modules:
  0.0 63.3 jit_solution(5880381639255920283)
XLA Ops:
  0.0 0.0 copy-start.3
  0.0 0.0 copy-start.2
  0.7 0.0 copy-done.3
  0.7 0.0 copy-done.2
  0.7 0.0 copy-start
  0.7 0.7 %copy-done = f32[1,32,256]{2,1,0:T(8,128)S(1)} copy-done((f32[1,32,256]{2,1,0:T(8,128)S(1)}, f32[1,32,256]{2,1,0:T(8,128)}, u32[]{:S(2)}) %copy-start) | copy-done | bytes 32792
  1.5 0.0 copy-start.1
  1.5 0.8 %copy-done.1 = bf16[64,256]{1,0:T(8,128)(2,1)S(1)} copy-done((bf16[64,256]{1,0:T(8,128)(2,1)S(1)}, bf16[64,256]{1,0:T(8,128)(2,1)}, u32[]{:S(2)}) %copy-start.1) | copy-done | bytes 32792
  2.2 60.4 %shard_map.55 = f32[64,256]{1,0:T(8,128)S(1)} custom-call(f32[1,32,256]{2,1,0:T(8,128)S(1)} %copy-done, bf16[64,256]{1,0:T(8,128)(2,1)S(1)} %copy-done.1, f32[1]{0:T(128)S(6)} %copy.7.scale_in, s32[2,24]{1,0:T(2,128)S(1)} %copy-done.2, s32[2]{0:T(128)S(1)} %copy-done.3), custom_call_target="tpu_custom_call" | custom-call | tf_op jit(solution)/shard_map/pallas_call | solution.py:405
  62.7 0.6 copy.8
Async XLA Ops:
  0.0 0.7 %copy-start.3 = (s32[2]{0:T(128)S(1)}, s32[2]{0:T(128)}, u32[]{:S(2)}) copy-start(s32[2]{0:T(128)} %counts_in.1) | copy-start | bytes 28
  0.0 0.7 %copy-start.2 = (s32[2,24]{1,0:T(2,128)S(1)}, s32[2,24]{1,0:T(2,128)}, u32[]{:S(2)}) copy-start(s32[2,24]{1,0:T(2,128)} %lists_in.1) | copy-start | bytes 580
  0.7 0.8 %copy-start = (f32[1,32,256]{2,1,0:T(8,128)S(1)}, f32[1,32,256]{2,1,0:T(8,128)}, u32[]{:S(2)}) copy-start(f32[1,32,256]{2,1,0:T(8,128)} %states.1) | copy-start | bytes 98308
  1.5 0.8 %copy-start.1 = (bf16[64,256]{1,0:T(8,128)(2,1)S(1)}, bf16[64,256]{1,0:T(8,128)(2,1)}, u32[]{:S(2)}) copy-start(bf16[64,256]{1,0:T(8,128)(2,1)} %vectors.1) | copy-start | bytes 98308

commit v3 on v2

--- a/solution.py
+++ b/solution.py
@@ -10,9 +10,7 @@
 
 MESH = pl.DeviceIdType.MESH
 BLK = 128
-FO = 0
-SO = 3
-VL = 32
+VMEM_KIB = 55170
 STEP = 5461.0
 NONE = -1
 
@@ -226,14 +224,7 @@
     ls = (ls_all, ls_send, ls_recv)
     sc = (sc_all, sc_send, sc_recv)
     near, far = near_first[:-1], near_first[-1]
-    if FO == 0:
-        first_steps = [(w, d) for w in ("st", "ls", "ve") for d in hops + [0]]
-    elif FO == 1:
-        first_steps = [("st", d) for d in hops] + [("ls", d) for d in hops] + [("st", 0), ("ls", 0)] + [("ve", d) for d in hops + [0]]
-    elif FO == 2:
-        first_steps = [("st", far), ("ls", far), ("ve", far)] + [(w, d) for w in ("st", "ls") for d in near + [0]] + [("ve", d) for d in near + [0]]
-    elif FO == 3:
-        first_steps = [("st", far), ("ls", far)] + [(w, d) for w in ("st", "ls") for d in near + [0]] + [("ve", d) for d in [0] + near + [far]]
+    first_steps = [(w, d) for w in ("st", "ls", "ve") for d in hops + [0]]
     for what, d in first_steps:
         group = {"st": st, "ls": ls, "ve": (ve_all, ve_send.at[0], ve_recv)}[what]
         if d:
@@ -299,14 +290,9 @@
                 )
             total[:, part] = sums
 
-    if SO == 0:
-        second_steps = [("fs", d) for d in near] + [("b0", 0), ("b", 0), ("fs", far)] + [("b", d) for d in near] + [("fv", d) for d in near] + [("p", 0), ("b", far), ("fv", far)] + [("p", d) for d in near]
-    elif SO == 1:
-        second_steps = [("fs", d) for d in near] + [("b0", 0), ("b", 0)] + [("b", d) for d in near] + [("fs", far)] + [("fv", d) for d in near] + [("p", 0), ("b", far), ("fv", far)] + [("p", d) for d in near]
-    elif SO == 2:
-        second_steps = [("fs", d) for d in near] + [("b0", 0), ("b", 0), ("fs", far), ("fv", near[0])] + [("b", d) for d in near] + [("fv", near[-1])] + [("p", 0), ("fv", far), ("b", far)] + [("p", d) for d in near]
-    elif SO == 3:
-        second_steps = [("fs", d) for d in near] + [("b0", 0), ("b", 0), ("fs", far)] + [("fv", d) for d in near] + [("b", d) for d in near] + [("fv", far), ("p", 0), ("b", far)] + [("p", d) for d in near]
+    second_steps = [("fs", d) for d in near] + [("b0", 0), ("b", 0), ("fs", far)]
+    second_steps += [("fv", d) for d in near] + [("b", d) for d in near[:1]] + [("fv", far)]
+    second_steps += [("b", d) for d in near[1:]] + [("p", 0), ("b", far)] + [("p", d) for d in near]
     for step, dz in second_steps:
         if step == "fs":
             forward(*st, dz)
@@ -331,13 +317,26 @@
     swap_1.wait_recv()
     sums = jnp.sum(row_sum[:, :own] + px_in[0, vecs:], axis=0, keepdims=True)
     sc_all[chip] = ((total[:, :own] + px_in[0, :vecs]) / (sums * sums)).astype(jnp.bfloat16)
-    for d in hops:
-        send_z(*sc, d)
+    @pl.when(zh == 0)
+    def _first_group():
+        for d in hops:
+            send_z(*sc, d)
+
+    @pl.when(zh > 0)
+    def _to_first_group():
+        send_z(*sc, side - zh)
+
     send_y(*sc)
     total[...] = jnp.zeros_like(total)
+    products(sc_all, shard_wait, second, 0)
+
+    @pl.when(zh > 0)
+    def _to_others():
+        for k in range(1, side - 1):
+            send_z(*sc, (k + (k >= zh).astype(jnp.int32) - zh) % side)
+
     for dz in near:
         forward(*sc, dz)
-    products(sc_all, shard_wait, second, 0)
     forward(*sc, far)
     for dz in near:
         products(sc_all, shard_wait, second, dz)
@@ -404,7 +403,7 @@
     dma = pltpu.SemaphoreType.DMA
     return pl.pallas_call(
         functools.partial(kernel, side, xs, slices),
-        out_shape=jax.ShapeDtypeStruct((vecs, own), jnp.float32),
+        out_shape=pltpu.VMEM((vecs, own), jnp.float32),
         in_specs=[hbm] * 5,
         out_specs=vmem,
         scratch_shapes=[
@@ -449,7 +448,7 @@
             dma((5,)),
         ],
         compiler_params=pltpu.CompilerParams(
-            collective_id=0, has_side_effects=True, vmem_limit_bytes=VL * 1024 * 1024
+            collective_id=0, has_side_effects=True, vmem_limit_bytes=VMEM_KIB * 1024
         ),
     )(states, vectors, kernel_scale, neighbour_blocks, neighbour_count)
 

time: 63.5 us -> 59.6 us (0.939)
  Pallas kernels: 60.4 us -> 58.1 us
  local copies, waits for them, and re-layouts: 2.15 us -> 0.63 us
    pallas_call x1, Pallas kernels: 60.4 us -> 58.1 us  [per_device(): pl.pallas_call(functools.partial(kernel, side, xs, slices), out_shape=plt...]
    unnamed x9 -> x1, local copies, waits for them, and re-layouts: 2.15 us -> 0.63 us
where the time goes in v3:
time: 59.6 us; the launch traced here: 59.4 us
  Pallas kernels  58.1 us (97%)
  between operations  0.66 us (1%)
  local copies, waits for them, and re-layouts  0.63 us (1%)
    pallas_call x1, Pallas kernels, per_device(): pl.pallas_call(functools.partial(kernel, side, xs, slices), out_shape=plt...  58.1 us

profile of v3, /device:TPU:1, one launch (start us, length us, event | category | flops | bytes accessed | tf_op | source)
XLA Modules:
  0.0 59.4 jit_solution(3788667207222336977)
XLA Ops:
  0.7 58.1 %shard_map.55 = f32[64,256]{1,0:T(8,128)S(1)} custom-call(f32[1,32,256]{2,1,0:T(8,128)} %states.1, bf16[64,256]{1,0:T(8,128)(2,1)} %vectors.1, f32[1]{0:T(128)S(6)} %copy.8.scale_in, s32[2,24]{1,0:T(2,128)} %lists_in.1, s32[2]{0:T(128)} %counts_in.1), custom_call_target="tpu_custom_call" | custom-call | tf_op jit(solution)/shard_map/pallas_call | solution.py:404
  58.8 0.6 %copy.7 = f32[64,256]{1,0:T(8,128)} copy(f32[64,256]{1,0:T(8,128)S(1)} %shard_map.55) | data formatting | bytes 131072

commit v4 on v3

--- a/solution.py
+++ b/solution.py
@@ -354,11 +354,28 @@
         rows, lanes = slice(t // wide * 8, t // wide * 8 + 8), slice(t % wide * 128, t % wide * 128 + 128)
         rs_out[t] = total[rows, lanes] + px_in[1, rows, lanes]
 
-    for d in range(1, slices):
-        there = (tm + d) % slices
+    def scatter(there):
         copy(
-            rs_out.at[pl.ds(there * per, per)], rs_in.at[tm], rs_send, rs_recv.at[tm], at_slice(d)
+            rs_out.at[pl.ds(there * per, per)],
+            rs_in.at[tm],
+            rs_send,
+            rs_recv.at[tm],
+            {"traj": traj, "tm": there},
         ).start()
+
+    def far_first(send):
+        runs = slices // xs
+        across = sorted(range(xs), key=lambda d: -min(d, xs - d))
+        for k in range(runs):
+            run = jnp.where(2 * zl >= runs, k, runs - 1 - k)
+            for d in across:
+                there = run * xs + (x + d) % xs
+                if d:
+                    send(there)
+                else:
+                    pl.when(run != zl)(functools.partial(send, there))
+
+    far_first(scatter)
 
     def scattered(d, carry):
         there = (tm + d) % slices
@@ -369,8 +386,12 @@
     lax.fori_loop(1, slices, scattered, 0)
     ag[tm] = jnp.sum(rs_in[...], axis=0)
 
-    for d in range(1, slices):
-        copy(ag.at[tm], ag.at[tm], ag_send, ag_recv.at[tm], at_slice(d)).start()
+    def spread(there):
+        copy(
+            ag.at[tm], ag.at[tm], ag_send, ag_recv.at[tm], {"traj": traj, "tm": there}
+        ).start()
+
+    far_first(spread)
 
     def arrived(d, carry):
         there = (tm + d) % slices

time: 59.6 us -> 58.9 us (0.988)
  Pallas kernels: 58.1 us -> 57.3 us
    pallas_call x1, Pallas kernels: 58.1 us -> 57.3 us  [per_device(): pl.pallas_call(functools.partial(kernel, side, xs, slices), out_shape=plt...]
where the time goes in v4:
time: 58.9 us; the launch traced here: 58.6 us
  Pallas kernels  57.3 us (97%)
  between operations  0.66 us (1%)
  local copies, waits for them, and re-layouts  0.63 us (1%)
    pallas_call x1, Pallas kernels, per_device(): pl.pallas_call(functools.partial(kernel, side, xs, slices), out_shape=plt...  57.3 us

profile of v4, /device:TPU:1, one launch (start us, length us, event | category | flops | bytes accessed | tf_op | source)
XLA Modules:
  0.0 58.6 jit_solution(3847913516272441811)
XLA Ops:
  0.7 57.3 %shard_map.55 = f32[64,256]{1,0:T(8,128)S(1)} custom-call(f32[1,32,256]{2,1,0:T(8,128)} %states.1, bf16[64,256]{1,0:T(8,128)(2,1)} %vectors.1, f32[1]{0:T(128)S(6)} %copy.8.scale_in, s32[2,24]{1,0:T(2,128)} %lists_in.1, s32[2]{0:T(128)} %counts_in.1), custom_call_target="tpu_custom_call" | custom-call | tf_op jit(solution)/shard_map/pallas_call | solution.py:425
  57.9 0.6 %copy.7 = f32[64,256]{1,0:T(8,128)} copy(f32[64,256]{1,0:T(8,128)S(1)} %shard_map.55) | data formatting | bytes 131072

commit v5 on v4

--- a/solution.py
+++ b/solution.py
@@ -392,17 +392,6 @@
         ).start()
 
     far_first(spread)
-
-    def arrived(d, carry):
-        there = (tm + d) % slices
-        wait_for(ag.at[there], ag_recv.at[there])
-        return carry
-
-    lax.fori_loop(1, slices, arrived, 0)
-    for t in range(tiles):
-        rows, lanes = slice(t // wide * 8, t // wide * 8 + 8), slice(t % wide * 128, t % wide * 128 + 128)
-        out[rows, lanes] = ag[t // per, t % per]
-
     all_sent(st_all, st_send)
     all_sent(ls_all, ls_send)
     shares_sent()
@@ -411,6 +400,17 @@
         swap.wait_send()
 
     wait_for(rs_in.at[pl.ds(0, slices - 1)], rs_send)
+
+    def arrived(d, carry):
+        there = (tm + d) % slices
+        wait_for(ag.at[there], ag_recv.at[there])
+        return carry
+
+    lax.fori_loop(1, slices, arrived, 0)
+    for t in range(tiles):
+        rows, lanes = slice(t // wide * 8, t // wide * 8 + 8), slice(t % wide * 128, t % wide * 128 + 128)
+        out[rows, lanes] = ag[t // per, t % per]
+
     wait_for(ag.at[pl.ds(0, slices - 1)], ag_send)
 
 

time: 58.9 us -> 58.9 us (level)
  no operation moved by 1% of the time
where the time goes in v5:
time: 58.9 us; the launch traced here: 58.5 us
  Pallas kernels  57.3 us (97%)
  between operations  0.66 us (1%)
  local copies, waits for them, and re-layouts  0.63 us (1%)
    pallas_call x1, Pallas kernels, per_device(): pl.pallas_call(functools.partial(kernel, side, xs, slices), out_shape=plt...  57.3 us

profile of v5, /device:TPU:1, one launch (start us, length us, event | category | flops | bytes accessed | tf_op | source)
XLA Modules:
  0.0 58.5 jit_solution(9254076612335132655)
XLA Ops:
  0.7 57.3 %shard_map.55 = f32[64,256]{1,0:T(8,128)S(1)} custom-call(f32[1,32,256]{2,1,0:T(8,128)} %states.1, bf16[64,256]{1,0:T(8,128)(2,1)} %vectors.1, f32[1]{0:T(128)S(6)} %copy.8.scale_in, s32[2,24]{1,0:T(2,128)} %lists_in.1, s32[2]{0:T(128)} %counts_in.1), custom_call_target="tpu_custom_call" | custom-call | tf_op jit(solution)/shard_map/pallas_call | solution.py:425
  57.9 0.6 %copy.7 = f32[64,256]{1,0:T(8,128)} copy(f32[64,256]{1,0:T(8,128)S(1)} %shard_map.55) | data formatting | bytes 131072
